TPU v7x, 32 devices: a whole 2x2x4 slice. The times are simulated.
32 devices in a mesh: enc: 2 (over core), row: 4 (over y, x), col: 4 (over z).
Axes of the slice: x: 2, y: 2, z: 4, core: 2. Of those that a mesh axis runs over, the one named last changes fastest.
Arguments:
- embedding: bfloat16 [16, 256, 256], P(('row', 'col'), 'enc'), may hold values from -6 to 6
- w_first: bfloat16 [256, 256], replicated, may hold values from -0.375 to 0.375
- b_first: float32 [256], replicated, may hold values from -3 to 3
- w_second: bfloat16 [256, 256], replicated, may hold values from -0.375 to 0.375
- w_layer: bfloat16 [256, 256], replicated, may hold values from -0.375 to 0.375
- block_source: int32 [16, 48], P(('row', 'col')), may hold values from 0 to 15, as said below
- block_rows: int32 [16, 48], P(('row', 'col')), may hold values from 0 to 1
- block_cols: int32 [16, 48], P(('row', 'col')), may hold values from 0 to 1
- block_count: int32 [16], P(('row', 'col')), may hold values from 3 to 48, as said below
- block_tiles: bfloat16 [16, 48, 128, 128], P(('row', 'col')), may hold values from -0.15625 to 0.15625
- node_order: int32 [4, 4, 256], P(None, 'col'), may hold values from 0 to 255, each once within a row
- cotangent: bfloat16 [16, 256, 256], P(('row', 'col'), None, 'enc'), may hold values from -9 to 9
Outputs:
- activated: bfloat16 [16, 256, 256], P(('row', 'col'), None, 'enc')
- grad_layer: float32 [256, 256], replicated
- grad_embed: float32 [16, 256, 256], P(('row', 'col'), 'enc')
Inputs may be any that keep to these rules, and one draw needn't show every extreme that they name: `block_source`: the slots of target s come in 16 runs of 3 slots; the slots of one run name the same source segment, different runs name different ones, and the first run names s itself. `block_count`: at least one target segment has all 48 slots live.
All inputs are finite; a program needn't handle non-finite values.
Results may differ from a plain program's by a relative error of at most 0.01.
Values may be sent and summed in bfloat16 or wider, within the bound.
A program may use at most 128 MiB of HBM per device.

v0:
```python
import jax
import jax.numpy as jnp
from jax import lax
from jax.sharding import PartitionSpec as P


def silu_slope(values):
    sigmoid = jax.nn.sigmoid(values)
    return sigmoid * (1.0 + values * (1.0 - sigmoid))


def segment_ids(seg_total, row_devices, col_devices):
    position = jnp.arange(seg_total, dtype=jnp.int32)
    return position % row_devices * col_devices + position // row_devices


def pick_slots(carry, piece, seg_ids, slot_src, slot_cols, row_blocks, tile_size):
    seg_total = seg_ids.shape[0]
    blocks = piece.reshape(seg_total * row_blocks, tile_size, piece.shape[-1])
    match = slot_src[:, None] == seg_ids[None, :]
    inside = jnp.any(match, axis=1)
    local = jnp.sum(jnp.where(match, jnp.arange(seg_total, dtype=jnp.int32)[None, :], 0), axis=1)
    chosen = jnp.take(blocks, local * row_blocks + slot_cols, axis=0)
    return jnp.where(inside[:, None, None], chosen, carry)


def aggregate_slots(picked, slot_rows, live_mask, slot_tiles, row_blocks):
    products = jnp.einsum("lij,ljf->lif", slot_tiles, picked, preferred_element_type=jnp.float32)
    row_pick = jax.nn.one_hot(slot_rows, row_blocks, dtype=jnp.float32) * live_mask[:, None]
    return jnp.einsum("lr,lif->rif", row_pick, products, precision=lax.Precision.HIGHEST)


def place_terms(products, global_block, row_count, tile_size):
    block_total = row_count // tile_size
    local = global_block
    inside = (local >= 0) & (local < block_total)
    local = jnp.where(inside, local, block_total)
    placed = jnp.zeros((block_total, tile_size, products.shape[-1]), jnp.float32)
    placed = placed.at[local].add(products, mode="drop")
    return placed.reshape(row_count, products.shape[-1])


def invert_order(orders):
    positions = jnp.broadcast_to(
        jnp.arange(orders.shape[1], dtype=jnp.int32)[None, :], orders.shape
    )
    seg_index = jnp.arange(orders.shape[0], dtype=jnp.int32)[:, None]
    return jnp.zeros(orders.shape, jnp.int32).at[seg_index, orders].set(positions)


def on_device(
    embedding,
    w_first,
    b_first,
    w_second,
    w_layer,
    block_source,
    block_rows,
    block_cols,
    block_count,
    block_tiles,
    node_order,
    cotangent,
):
    enc_rows = embedding[0]
    half_rows = enc_rows.shape[0]
    full_width = enc_rows.shape[1]
    seg_rows = 2 * half_rows
    half_width = full_width // 2
    tile_size = block_tiles.shape[-1]
    row_blocks = seg_rows // tile_size
    row_devices = lax.axis_size("row")
    col_devices = lax.axis_size("col")
    enc_index = lax.axis_index("enc")
    slot_src = block_source[0]
    slot_rows = block_rows[0]
    slot_cols = block_cols[0]
    slot_tiles = block_tiles[0]
    slot_total = slot_src.shape[0]
    live_mask = (jnp.arange(slot_total, dtype=jnp.int32) < block_count[0]).astype(jnp.float32)
    first_linear = jnp.dot(enc_rows, w_first, preferred_element_type=jnp.float32) + b_first
    hidden_first = jax.nn.silu(first_linear).astype(jnp.bfloat16)
    encoded = jnp.dot(hidden_first, w_second, preferred_element_type=jnp.float32).astype(
        jnp.bfloat16
    )
    projected = jnp.dot(encoded, w_layer, preferred_element_type=jnp.float32).astype(jnp.bfloat16)
    stripe_perm = node_order[:, 0, :]
    gathered = lax.all_gather(projected, ("enc", "row"), axis=0, tiled=True)
    stacked = gathered.reshape(2, row_devices, half_rows, full_width).transpose(1, 0, 2, 3)
    stacked = stacked.reshape(row_devices, seg_rows, full_width)
    own_half = lax.dynamic_slice_in_dim(stacked, enc_index * half_width, half_width, 2)
    stripe_panel = jnp.take_along_axis(own_half, stripe_perm[:, :, None], axis=1)
    stripe_panel = stripe_panel.reshape(row_devices * seg_rows, half_width)
    empty = jnp.zeros((slot_total, tile_size, half_width), jnp.bfloat16)
    panel_piece = lax.all_gather(stripe_panel, "col", axis=0, tiled=True)
    seg_ids = segment_ids(panel_piece.shape[0] // seg_rows, row_devices, col_devices)
    picked = pick_slots(empty, panel_piece, seg_ids, slot_src, slot_cols, row_blocks, tile_size)
    aggregated = aggregate_slots(picked, slot_rows, live_mask, slot_tiles, row_blocks)
    aggregated = aggregated.reshape(seg_rows, half_width)
    activated = jax.nn.silu(aggregated).astype(jnp.bfloat16)
    pre_grad = (cotangent[0].astype(jnp.float32) * silu_slope(aggregated)).astype(jnp.bfloat16)
    own_blocks = pre_grad.reshape(row_blocks, tile_size, half_width)
    gathered_grad = jnp.take(own_blocks, slot_rows, axis=0)
    back_products = jnp.einsum(
        "lji,ljf->lif", slot_tiles, gathered_grad, preferred_element_type=jnp.float32
    )
    back_products = back_products * live_mask[:, None, None]
    source_row = slot_src // col_devices
    source_col = slot_src % col_devices
    global_block = (source_col * row_devices + source_row) * row_blocks + slot_cols
    partials = lax.psum_scatter(
        place_terms(
            back_products, global_block, lax.axis_size("col") * (row_devices * seg_rows), tile_size
        ),
        "col",
        scatter_dimension=0,
        tiled=True,
    )
    inverse = invert_order(stripe_perm)
    node_terms = jnp.take_along_axis(
        partials.reshape(row_devices, seg_rows, half_width), inverse[:, :, None], axis=1
    )
    by_core = node_terms.reshape(row_devices, 2, half_rows, half_width).transpose(1, 0, 2, 3)
    enc_weight = enc_index.astype(jnp.float32)
    widened = jnp.concatenate([by_core * (1.0 - enc_weight), by_core * enc_weight], axis=3)
    widened = widened.reshape(2 * row_devices * half_rows, full_width)
    node_grad = lax.psum_scatter(widened, ("enc", "row"), scatter_dimension=0, tiled=True)
    projected_grad = node_grad.astype(jnp.bfloat16)
    grad_part = lax.dot_general(
        encoded, projected_grad, (((0,), (0,)), ((), ())), preferred_element_type=jnp.float32
    )
    grad_layer = lax.psum(grad_part, ("enc", "row", "col"))
    encoded_grad = lax.dot_general(
        projected_grad, w_layer, (((1,), (1,)), ((), ())), preferred_element_type=jnp.float32
    ).astype(jnp.bfloat16)
    hidden_grad = lax.dot_general(
        encoded_grad, w_second, (((1,), (1,)), ((), ())), preferred_element_type=jnp.float32
    )
    hidden_grad = (hidden_grad * silu_slope(first_linear)).astype(jnp.bfloat16)
    grad_embed = lax.dot_general(
        hidden_grad, w_first, (((1,), (1,)), ((), ())), preferred_element_type=jnp.float32
    )
    return (activated[None], grad_layer, grad_embed[None])


def solution(mesh):
    in_specs = (
        P(("row", "col"), "enc", None),
        P(),
        P(),
        P(),
        P(),
        P(("row", "col"), None),
        P(("row", "col"), None),
        P(("row", "col"), None),
        P(("row", "col")),
        P(("row", "col"), None, None, None),
        P(None, "col", None),
        P(("row", "col"), None, "enc"),
    )
    out_specs = (P(("row", "col"), None, "enc"), P(), P(("row", "col"), "enc", None))
    return jax.shard_map(
        on_device, mesh=mesh, in_specs=in_specs, out_specs=out_specs, check_vma=False
    )
```

profile of v0, /device:TPU:0, one launch (start us, length us, event | category | flops | bytes accessed | tf_op | source)
XLA Modules:
  0.0 336.5 jit_solution(1646990656992906335)
XLA Ops:
  7.2 0.0 copy-start
  7.2 0.0 all-gather.2.cloned.1.call-start
  7.2 0.8 shift-left_or_fusion
  8.0 0.7 compare_and_fusion
  8.7 1.1 convolution_add_fusion
  9.8 1.1 convolution_convert_fusion.2
  10.9 1.1 convolution_convert_fusion.1
  12.0 26.1 %all_gather.6 = bf16[1024,256]{1,0:T(8,128)(2,1)S(1)} all-gather(bf16[128,256]{1,0:T(8,128)(2,1)S(1)} %convolution_convert_fusion.1), channel_id=1, replica_groups=mesh['enc'=2,'row'=4,'col'=4] {'enc','row'}, dimensions={0}, use_global_device_ids=true | all-gather | bytes 589824 | tf_op jit(solution)/shard_map/all_gather | solution.py:88
  38.1 0.1 constant_dynamic-slice_fusion
  38.2 0.0 copy-start.6
  38.2 5.8 %gather_fusion.2 = bf16[1024,128]{1,0:T(8,128)(2,1)S(1)} fusion(bf16[4,256,128]{2,1,0:T(8,128)(2,1)S(1)} %constant_dynamic-slice_fusion, s32[1024]{0:T(1024)S(1)} %bitcast.113), kind=kCustom, calls=%fused_computation.2 | custom fusion | bytes 532480 | tf_op jit(solution)/shard_map/jit(take_along_axis)/gather | solution.py:92
  44.0 0.9 broadcast_select_fusion
  45.0 0.0 all-gather.2.cloned.1.call-update
  45.0 0.0 reduce-scatter.3.cloned.1.call-start
  45.7 0.1 fusion.23
  45.9 0.1 compare_reduce_fusion
  46.0 0.5 compare_and_fusion.1
  46.5 27.5 %all-gather.2.cloned.1.call-done = bf16[4096,128]{1,0:T(8,128)(2,1)} async-done(((bf16[1024,128]{1,0:T(8,128)(2,1)}), bf16[4096,128]{1,0:T(8,128)(2,1)}) %all-gather.2.cloned.1.call-update) | async-done | bytes 1048592 | tf_op jit(solution)/shard_map/all_gather | solution.py:95
  74.0 2.1 gather_fusion
  76.1 3.1 convolution_bitcast_fusion
  79.2 3.6 %copy.36 = f32[48,128,128]{2,0,1:T(8,128)} copy(f32[48,128,128]{1,2,0:T(8,128)} %convolution_bitcast_fusion) | data formatting | bytes 6291456 | tf_op jit(solution)/shard_map/lij,ljf->lif/dot_general | solution.py:28
  82.8 3.5 %fusion.27 = f32[2,128,128]{2,0,1:T(2,128)S(1)} fusion(f32[48,128,128]{2,0,1:T(8,128)} %copy.36, f32[48]{0:T(128)S(1)} %get-tuple-element.12, s32[48]{0:T(128)S(1)} %bitcast.126), kind=kOutput, calls=%fused_computation.85 | convolution fusion | flops 18874560 | bytes 3277184 | tf_op jit(solution)/shard_map/lr,lif->rif/dot_general | solution.py:30
  86.3 0.1 fusion.12
  86.4 0.8 gather_fusion.1
  87.2 3.2 multiply_bitcast_fusion
  90.4 3.5 %copy.41 = f32[48,128,128]{2,1,0:T(8,128)} copy(f32[48,128,128]{1,2,0:T(8,128)} %multiply_bitcast_fusion) | data formatting | bytes 6291456 | tf_op jit(solution)/shard_map/mul | solution.py:107
  94.0 1.6 broadcast_in_dim.103
  95.6 10.0 %scatter_fusion = f32[32,128,128]{2,1,0:T(8,128)} fusion(f32[32,128,128]{2,1,0:T(8,128)} %broadcast_in_dim.103, s32[48]{0:T(128)S(1)} %get-tuple-element.9, f32[48,128,128]{2,1,0:T(8,128)} %copy.41), kind=kCustom, calls=%fused_computation.4 | custom fusion | flops 786432 | bytes 9437376 | tf_op jit(solution)/shard_map/scatter-add | solution.py:39
  105.6 0.0 reduce-scatter.3.cloned.1.call-update
  105.6 0.0 reduce-scatter.5.cloned.1.call-start
  105.7 0.5 copy-done.8
  106.2 0.1 multiply_reduce_fusion
  106.3 0.1 and_reduce_fusion
  106.4 4.3 %scatter_custom_fusion.1 = s32[1024]{0:T(1024)S(1)} fusion(s32[1024]{0:T(1024)S(1)} %bitcast.125, s32[1024]{0:T(1024)S(1)} %bitcast.124, s32[]{:T(128)} %constant.117.clone.1), kind=kCustom, calls=%fused_computation.70 | custom fusion | bytes 4100
  110.8 38.3 %reduce-scatter.3.cloned.1.call-done = f32[1024,128]{1,0:T(8,128)} async-done(((f32[4096,128]{1,0:T(8,128)}), f32[1024,128]{1,0:T(8,128)}) %reduce-scatter.3.cloned.1.call-update) | async-done | bytes 524304 | tf_op jit(solution)/shard_map/reduce_scatter | solution.py:111
  149.1 10.6 %gather_fusion.3 = f32[1024,128]{1,0:T(8,128)S(1)} fusion(f32[4,256,128]{2,1,0:T(8,128)} %bitcast.114, s32[1024]{0:T(1024)S(1)} %bitcast.112), kind=kCustom, calls=%fused_computation.3 | custom fusion | bytes 1056768 | tf_op jit(solution)/shard_map/jit(take_along_axis)/gather | solution.py:120
  159.7 0.2 multiply_bitcast_fusion.2
  159.9 1.0 pad_maximum_fusion
  161.0 0.0 reduce-scatter.5.cloned.1.call-update
  161.0 0.0 all-reduce.2.cloned.1.call-start
  161.0 0.7 fusion.16
  161.7 34.8 %reduce-scatter.5.cloned.1.call-done = f32[128,256]{1,0:T(8,128)} async-done(((f32[1024,256]{1,0:T(8,128)}), f32[128,256]{1,0:T(8,128)}) %reduce-scatter.5.cloned.1.call-update) | async-done | bytes 131088 | tf_op jit(solution)/shard_map/reduce_scatter | solution.py:127
  196.5 1.8 fusion.21
  198.3 0.0 all-reduce.2.cloned.1.call-update
  198.3 1.2 fusion.8
  199.6 0.9 convolution_bitcast_fusion.1
  200.4 127.9 %all-reduce.2.cloned.1.call-done = f32[256,256]{1,0:T(8,128)} async-done(((f32[256,256]{1,0:T(8,128)}), f32[256,256]{1,0:T(8,128)}) %all-reduce.2.cloned.1.call-update) | async-done | bytes 262160 | tf_op jit(solution)/shard_map/psum | solution.py:132
  328.3 1.7 copy.57
  (33 shorter events, 0.2 us)
Async XLA Ops:
  7.2 68.9 %copy-start = (bf16[1,48,128,128]{3,2,1,0:T(8,128)(2,1)S(1)}, bf16[1,48,128,128]{3,2,1,0:T(8,128)(2,1)}, u32[]{:S(2)}) copy-start(bf16[1,48,128,128]{3,2,1,0:T(8,128)(2,1)} %param.21) | copy-start | bytes 4718596
  7.2 66.8 %all-gather.2.cloned.1.call-start = ((), (), s32[]{:S(2)}) async-start(), calls=%async_computation.2 | async-start | bytes 1310720 | tf_op jit(solution)/shard_map/all_gather | solution.py:95
  38.2 7.5 %copy-start.4 = (s32[1,48]{1,0:T(1,128)S(1)}, s32[1,48]{1,0:T(1,128)}, u32[]{:S(2)}) copy-start(s32[1,48]{1,0:T(1,128)} %param.18) | copy-start | bytes 580
  38.2 7.5 %copy-start.5 = (s32[1,48]{1,0:T(1,128)S(1)}, s32[1,48]{1,0:T(1,128)}, u32[]{:S(2)}) copy-start(s32[1,48]{1,0:T(1,128)} %param.17) | copy-start | bytes 580
  38.2 7.6 %copy-start.6 = (s32[1,48]{1,0:T(1,128)S(1)}, s32[1,48]{1,0:T(1,128)}, u32[]{:S(2)}) copy-start(s32[1,48]{1,0:T(1,128)} %param.19) | copy-start | bytes 580
  45.0 104.1 %reduce-scatter.3.cloned.1.call-start = ((), (), s32[]{:S(2)}) async-start(), calls=%async_computation.3 | async-start | bytes 2621440 | tf_op jit(solution)/shard_map/reduce_scatter | solution.py:111
  82.8 3.5 %copy-start.3 = (bf16[1,256,128]{2,1,0:T(8,128)(2,1)S(1)}, bf16[1,256,128]{2,1,0:T(8,128)(2,1)}, u32[]{:S(2)}) copy-start(bf16[1,256,128]{2,1,0:T(8,128)(2,1)} %param.23) | copy-start | bytes 196612
  105.6 0.7 copy-start.8
  105.6 0.7 copy-start.7
  105.6 90.9 %reduce-scatter.5.cloned.1.call-start = ((), (), s32[]{:S(2)}) async-start(), calls=%async_computation.4 | async-start | bytes 1179648 | tf_op jit(solution)/shard_map/reduce_scatter | solution.py:127
  159.9 38.4 %copy-start.2 = (bf16[256,256]{1,0:T(8,128)(2,1)S(1)}, bf16[256,256]{1,0:T(8,128)(2,1)}, u32[]{:S(2)}) copy-start(bf16[256,256]{1,0:T(8,128)(2,1)} %param.16) | copy-start | bytes 393220
  159.9 38.4 %copy-start.9 = (bf16[256,256]{1,0:T(8,128)(2,1)S(1)}, bf16[256,256]{1,0:T(8,128)(2,1)}, u32[]{:S(2)}) copy-start(bf16[256,256]{1,0:T(8,128)(2,1)} %param.15) | copy-start | bytes 393220
  161.0 38.6 %copy-start.1 = (bf16[256,256]{1,0:T(8,128)(2,1)S(1)}, bf16[256,256]{1,0:T(8,128)(2,1)}, u32[]{:S(2)}) copy-start(bf16[256,256]{1,0:T(8,128)(2,1)} %param.13) | copy-start | bytes 393220
  161.0 167.4 %all-reduce.2.cloned.1.call-start = ((), (), s32[]{:S(2)}) async-start(), calls=%async_computation.5 | async-start | bytes 524288 | tf_op jit(solution)/shard_map/psum | solution.py:132
Sparse Core Ops, SparseCore 0:
  45.1 28.8 all-gather.1
  105.7 43.3 reduce-scatter.2
  161.1 35.3 reduce-scatter.4
  203.3 124.9 all-reduce.1
where the time goes:
time: 337 us
  waiting for transfers between devices  229 us (68%)
  local copies, waits for them, and re-layouts  34.7 us (10%)
  blocking collectives  26.1 us (8%)
  matrix products  16.9 us (5%)
  other arithmetic  15.4 us (5%)
  between operations  14.7 us (4%)
    psum x1, waiting for transfers between devices, on_device(): grad_layer = lax.psum(grad_part, ('enc', 'row', 'col'))  128 us
    reduce_scatter x1, waiting for transfers between devices, on_device(): lax.psum_scatter(place_terms(back_products, global_block, lax.axis_size('...  38.3 us
    reduce_scatter x1, waiting for transfers between devices, on_device(): lax.psum_scatter(widened, ('enc', 'row'), scatter_dimension=0, tiled=True)  34.8 us
    all_gather x1, waiting for transfers between devices, on_device(): panel_piece = lax.all_gather(stripe_panel, 'col', axis=0, tiled=True)  27.5 us
    all_gather x1, blocking collectives, on_device(): gathered = lax.all_gather(projected, ('enc', 'row'), axis=0, tiled=True)  26.1 us
    gather x1, local copies, waits for them, and re-layouts, on_device(): jnp.take_along_axis(partials.reshape(row_devices, seg_rows, half_width),...  10.6 us
    scatter-add x1, other arithmetic, place_terms(): placed = placed.at[local].add(products, mode='drop')  9.99 us
  transfers between devices with their start and end apart: 4, of which 4 were waited for; matrix products, arithmetic and copies ran while one was open for 2% of the time, Pallas kernels for 0%

commit v1 on v0

v1 whole, which is shorter than its diff:
```python
import functools

import jax
import jax.numpy as jnp
from jax import lax
from jax.experimental import pallas as pl
from jax.experimental.pallas import tpu as pltpu
from jax.sharding import PartitionSpec as P

MESH = pl.DeviceIdType.MESH
PAIR = 3
F32 = jnp.float32
BF16 = jnp.bfloat16


def silu_slope(values):
    sigmoid = jax.nn.sigmoid(values)
    return sigmoid * (1.0 + values * (1.0 - sigmoid))


def dot(a, b, ca=1, cb=0):
    return lax.dot_general(a, b, (((ca,), (cb,)), ((), ())), preferred_element_type=F32)


def kernel(n_row, n_col, emb, w1, b1, w2, wl, meta, tiles, order, cot,
           act_o, gl_o, ge_o,
           first, pall, psend, eall, pgx, pgsend, feat, acc, pgt, pb, rb, sb, cb, own,
           glp, glr, glc, glf,
           m_send, m_recv, fc_send, fr_send, f_recv, br_send, br_recv, bc_send, bc_recv,
           g1_send, g1_recv, g2_send, g2_recv, g3_send, g3_recv):
    me_e = lax.axis_index("enc")
    me_r = lax.axis_index("row")
    me_c = lax.axis_index("col")
    mate = 1 - me_e
    half = emb.shape[0]
    rows = 2 * half
    width = pall.shape[2]
    ts = tiles.shape[1]

    def row_of(d):
        return lax.rem(me_r + d, n_row)

    def col_of(d):
        return lax.rem(me_c + d, n_col)

    def remote(src, dst, ssem, rsem, **dev):
        return pltpu.make_async_remote_copy(
            src_ref=src, dst_ref=dst, send_sem=ssem, recv_sem=rsem,
            device_id=dev, device_id_type=MESH)

    barrier = pltpu.get_barrier_semaphore()
    pl.semaphore_signal(barrier, inc=1, device_id={"enc": mate}, device_id_type=MESH)
    for d in range(1, n_row):
        for e in range(2):
            pl.semaphore_signal(barrier, inc=1, device_id={"enc": e, "row": row_of(d)},
                                device_id_type=MESH)
    for d in range(1, n_col):
        pl.semaphore_signal(barrier, inc=1, device_id={"col": col_of(d)}, device_id_type=MESH)

    linear = dot(emb[...], w1[...]) + b1[...]
    first[...] = linear
    hidden = (linear * jax.nn.sigmoid(linear)).astype(BF16)
    encoded = dot(hidden, w2[...]).astype(BF16)
    eall[me_e] = encoded
    projected = dot(encoded, wl[...]).astype(BF16)
    psend[0] = projected[:, :width]
    psend[1] = projected[:, width:]
    pall[me_e] = psend[me_e]
    node_ids = lax.broadcasted_iota(jnp.int32, (rows, rows), 0)
    perm_t = jnp.where(node_ids == order[me_r], 1.0, 0.0).astype(BF16)

    pl.semaphore_wait(barrier, 2 * n_row - 1 + n_col - 1)
    copy_p = remote(psend.at[mate], pall.at[me_e], m_send.at[0], m_recv.at[0], enc=mate)
    copy_p.start()
    copy_e = remote(eall.at[me_e], eall.at[me_e], m_send.at[1], m_recv.at[1], enc=mate)
    copy_e.start()
    copy_p.wait()

    me_slot = me_r * n_col + me_c
    grid_own = dot(perm_t, pall[...].reshape(rows, width), 0, 0).astype(BF16)
    feat[me_slot] = grid_own.reshape(rows // ts, ts, width)

    def feat_col(d):
        slot = me_r * n_col + me_c
        return remote(feat.at[slot], feat.at[slot], fc_send.at[d], f_recv.at[slot], col=col_of(d))

    def feat_row(dc, dr):
        slot = me_r * n_col + col_of(dc)
        return remote(feat.at[slot], feat.at[slot], fr_send.at[dc * n_row + dr],
                      f_recv.at[slot], row=row_of(dr))

    def feat_wait(slot):
        remote(feat.at[slot], feat.at[slot], fc_send.at[0], f_recv.at[slot], enc=mate).wait_recv()

    for d in range(1, n_col):
        feat_col(d).start()
    for d in range(1, n_row):
        feat_row(0, d).start()

    def slots(seg):
        out = []
        for k in range(PAIR):
            m = meta[seg * PAIR + k]
            live = (m & 1) == 1
            out.append((m >> 3, live, (m >> 1) & 1, (m >> 2) & 1))
        return out

    def split(tile, live, which, axis):
        zero = jnp.zeros_like(tile)
        return jnp.concatenate(
            [jnp.where(jnp.logical_and(live, which == b), tile, zero) for b in range(rows // ts)],
            axis=axis)

    def pick(blocks, c):
        chosen = blocks[0]
        for b in range(1, len(blocks)):
            chosen = jnp.where(c == b, blocks[b], chosen)
        return chosen

    def forward(seg):
        lhs, rhs = [], []
        for index, live, r, c in slots(seg):
            lhs.append(split(tiles[index], live, r, 0))
            rhs.append(pick([feat[seg, b] for b in range(rows // ts)], c))
        return dot(jnp.concatenate(lhs, axis=1), jnp.concatenate(rhs, axis=0))

    acc[...] = forward(me_slot)

    def relay(dc, carry):
        slot = me_r * n_col + col_of(dc)
        feat_wait(slot)
        for d in range(1, n_row):
            feat_row(dc, d).start()
        acc[...] += forward(slot)
        return carry

    lax.fori_loop(1, n_col, relay, 0)

    def take(step, carry):
        dc = step // (n_row - 1)
        dr = step % (n_row - 1) + 1
        slot = row_of(dr) * n_col + col_of(dc)
        feat_wait(slot)
        acc[...] += forward(slot)
        return carry

    lax.fori_loop(0, n_col * (n_row - 1), take, 0)

    aggregated = acc[...]
    sig = jax.nn.sigmoid(aggregated)
    act_o[...] = (aggregated * sig).astype(BF16)
    slope = sig * (1.0 + aggregated * (1.0 - sig))
    pre = cot[...].astype(F32) * slope
    for b in range(rows // ts):
        pgt[b] = pre[b * ts:(b + 1) * ts].T.astype(BF16)

    def backward(seg):
        lhs, rhs = [], []
        for index, live, r, c in slots(seg):
            lhs.append(pgt[r])
            rhs.append(split(tiles[index], live, c, 1))
        return dot(jnp.concatenate(lhs, axis=1), jnp.concatenate(rhs, axis=0))

    def back_row(dc, dr):
        slot = row_of(dr) * n_col + col_of(dc)
        there = me_r * n_col + col_of(dc)
        return remote(pb.at[slot], rb.at[there], br_send.at[dc * n_row + dr],
                      br_recv.at[there], row=row_of(dr))

    def give(step, carry):
        dc = lax.rem(step // (n_row - 1) + 1, n_col)
        dr = step % (n_row - 1) + 1
        slot = row_of(dr) * n_col + col_of(dc)
        pb[slot] = backward(slot).astype(BF16)
        back_row(dc, dr).start()
        return carry

    lax.fori_loop(0, n_col * (n_row - 1), give, 0)

    def row_total(dc):
        total = backward(me_r * n_col + col_of(dc))
        for dr in range(1, n_row):
            slot = row_of(dr) * n_col + col_of(dc)
            remote(rb.at[slot], rb.at[slot], br_send.at[0], br_recv.at[slot], enc=mate).wait_recv()
            total = total + rb[slot].astype(F32)
        return total

    def back_col(dc):
        return remote(sb.at[dc], cb.at[me_c], bc_send.at[dc], bc_recv.at[me_c], col=col_of(dc))

    def pass_on(dc, carry):
        sb[dc] = row_total(dc).astype(BF16)
        back_col(dc).start()
        return carry

    lax.fori_loop(1, n_col, pass_on, 0)
    own[...] = row_total(0)

    def collect(dc, carry):
        at = col_of(dc)
        remote(cb.at[at], cb.at[at], bc_send.at[0], bc_recv.at[at], enc=mate).wait_recv()
        own[...] += cb[at].astype(F32)
        return carry

    lax.fori_loop(1, n_col, collect, 0)

    grid_grad = own[...].astype(BF16)
    node_grad = dot(perm_t, grid_grad, 1, 1).astype(BF16)
    pgsend[...] = node_grad.reshape(2, half, width)
    copy_g = remote(pgsend.at[mate], pgx.at[me_e], m_send.at[2], m_recv.at[2], enc=mate)
    copy_g.start()
    pgx[me_e] = pgsend[me_e]

    copy_e.wait()
    part = dot(eall[...].reshape(rows, eall.shape[2]), node_grad, 0, 0)
    chunk = glp.shape[1]
    glp[...] = part.astype(BF16).reshape(n_row, chunk, width)

    def gl_row(d):
        to = row_of(d)
        return remote(glp.at[to], glr.at[me_r], g1_send.at[d], g1_recv.at[me_r], row=to)

    for d in range(1, n_row):
        gl_row(d).start()

    copy_g.wait()
    full_grad = jnp.concatenate([pgx[0], pgx[1]], axis=1)
    encoded_grad = dot(full_grad, wl[...], 1, 1).astype(BF16)
    hidden_grad = (dot(encoded_grad, w2[...], 1, 1) * silu_slope(first[...])).astype(BF16)
    ge_o[...] = dot(hidden_grad, w1[...], 1, 1)

    total = glp[me_r].astype(F32)
    for d in range(1, n_row):
        at = row_of(d)
        remote(glr.at[at], glr.at[at], g1_send.at[0], g1_recv.at[at], enc=mate).wait_recv()
        total = total + glr[at].astype(F32)
    glc[me_c] = total.astype(BF16)

    def gl_col(d):
        return remote(glc.at[me_c], glc.at[me_c], g2_send.at[d], g2_recv.at[me_c], col=col_of(d))

    for d in range(1, n_col):
        gl_col(d).start()
    for d in range(1, n_col):
        at = col_of(d)
        remote(glc.at[at], glc.at[at], g2_send.at[0], g2_recv.at[at], enc=mate).wait_recv()
    total = glc[0].astype(F32)
    for c in range(1, n_col):
        total = total + glc[c].astype(F32)
    mine = me_e * n_row + me_r
    glf[mine] = total.astype(BF16)

    def gl_all(de, dr):
        return remote(glf.at[mine], glf.at[mine], g3_send.at[de * n_row + dr], g3_recv.at[mine],
                      enc=lax.rem(me_e + de, 2), row=row_of(dr))

    others = [(de, dr) for de in range(2) for dr in range(n_row) if de or dr]
    for de, dr in others:
        gl_all(de, dr).start()
    for de, dr in others:
        at = lax.rem(me_e + de, 2) * n_row + row_of(dr)
        remote(glf.at[at], glf.at[at], g3_send.at[0], g3_recv.at[at], enc=mate).wait_recv()
    for e in range(2):
        for r in range(n_row):
            gl_o[r * chunk:(r + 1) * chunk, e * width:(e + 1) * width] = (
                glf[e * n_row + r].astype(F32))

    for d in range(1, n_col):
        feat_col(d).wait_send()
        back_col(d).wait_send()
        gl_col(d).wait_send()
    for d in range(1, n_row):
        gl_row(d).wait_send()
    for de, dr in others:
        gl_all(de, dr).wait_send()

    def drain(step, carry):
        dc = step // (n_row - 1)
        dr = step % (n_row - 1) + 1
        feat_row(dc, dr).wait_send()
        back_row(dc, dr).wait_send()
        return carry

    lax.fori_loop(0, n_col * (n_row - 1), drain, 0)


def on_device(embedding, w_first, b_first, w_second, w_layer, block_source, block_rows,
              block_cols, block_count, block_tiles, node_order, cotangent):
    n_row = lax.axis_size("row")
    n_col = lax.axis_size("col")
    segs = n_row * n_col
    half = embedding.shape[1]
    full = embedding.shape[2]
    rows = 2 * half
    width = full // 2
    ts = block_tiles.shape[-1]
    blocks = rows // ts
    total = block_source.shape[1]

    slot = jnp.arange(total, dtype=jnp.int32)
    live = (slot < block_count[0]).astype(jnp.int32)
    value = (live + block_rows[0] * 2 + block_cols[0] * 4 + slot * 8).reshape(-1, PAIR)
    sources = block_source[0].reshape(-1, PAIR)
    match = sources[None, :, :] == jnp.arange(segs, dtype=jnp.int32)[:, None, None]
    meta = jnp.sum(jnp.where(match, value[None], 0), axis=1).reshape(segs * PAIR)

    vmem = pl.BlockSpec(memory_space=pltpu.VMEM)
    smem = pl.BlockSpec(memory_space=pltpu.SMEM)
    dma = pltpu.SemaphoreType.DMA
    chunk = full // n_row
    scratch = [
        pltpu.VMEM((half, full), F32),
        pltpu.VMEM((2, half, width), BF16),
        pltpu.VMEM((2, half, width), BF16),
        pltpu.VMEM((2, half, full), BF16),
        pltpu.VMEM((2, half, width), BF16),
        pltpu.VMEM((2, half, width), BF16),
        pltpu.VMEM((segs, blocks, ts, width), BF16),
        pltpu.VMEM((rows, width), F32),
        pltpu.VMEM((blocks, width, ts), BF16),
        pltpu.VMEM((segs, width, rows), BF16),
        pltpu.VMEM((segs, width, rows), BF16),
        pltpu.VMEM((n_col, width, rows), BF16),
        pltpu.VMEM((n_col, width, rows), BF16),
        pltpu.VMEM((width, rows), F32),
        pltpu.VMEM((n_row, chunk, width), BF16),
        pltpu.VMEM((n_row, chunk, width), BF16),
        pltpu.VMEM((n_col, chunk, width), BF16),
        pltpu.VMEM((2 * n_row, chunk, width), BF16),
        dma((3,)), dma((3,)),
        dma((n_col,)), dma((segs,)), dma((segs,)),
        dma((segs,)), dma((segs,)), dma((n_col,)), dma((n_col,)),
        dma((n_row,)), dma((n_row,)), dma((n_col,)), dma((n_col,)),
        dma((2 * n_row,)), dma((2 * n_row,)),
    ]
    activated, grad_layer, grad_embed = pl.pallas_call(
        functools.partial(kernel, n_row, n_col),
        out_shape=(
            jax.ShapeDtypeStruct((rows, width), BF16),
            jax.ShapeDtypeStruct((full, full), F32),
            jax.ShapeDtypeStruct((half, full), F32),
        ),
        in_specs=[vmem, vmem, vmem, vmem, vmem, smem, vmem, vmem, vmem],
        out_specs=(vmem, vmem, vmem),
        scratch_shapes=scratch,
        compiler_params=pltpu.CompilerParams(
            collective_id=0, has_side_effects=True, vmem_limit_bytes=48 * 1024 * 1024),
    )(embedding[0], w_first, b_first[None], w_second, w_layer, meta, block_tiles[0],
      node_order, cotangent[0])
    return (activated[None], grad_layer, grad_embed[None])


def solution(mesh):
    in_specs = (
        P(("row", "col"), "enc", None),
        P(),
        P(),
        P(),
        P(),
        P(("row", "col"), None),
        P(("row", "col"), None),
        P(("row", "col"), None),
        P(("row", "col")),
        P(("row", "col"), None, None, None),
        P(None, "col", None),
        P(("row", "col"), None, "enc"),
    )
    out_specs = (P(("row", "col"), None, "enc"), P(), P(("row", "col"), "enc", None))
    return jax.shard_map(
        on_device, mesh=mesh, in_specs=in_specs, out_specs=out_specs, check_vma=False
    )
```

time: 337 us -> 66.4 us (0.20)
  waiting for transfers between devices: 229 us -> 0 us
  Pallas kernels: 0 us -> 52.3 us
  blocking collectives: 26.1 us -> 0 us
  local copies, waits for them, and re-layouts: 34.7 us -> 10.3 us
  matrix products: 16.9 us -> 0 us
  between operations: 14.7 us -> 1.32 us
  other arithmetic: 15.4 us -> 2.19 us
    psum x1 -> x0, waiting for transfers between devices: 128 us -> none  [on_device(): grad_layer = lax.psum(grad_part, ('enc', 'row', 'col'))]
    reduce_scatter x2 -> x0, waiting for transfers between devices: 73.1 us -> none  [the longest x1 38.3 us: on_device(): lax.psum_scatter(place_terms(back_products, global_block, lax.axis_size('...]
    pallas_call x0 -> x1, Pallas kernels: none -> 52.3 us  [on_device(): pl.pallas_call(functools.partial(kernel, n_row, n_col), out_shape=(jax.Sh...]
    all_gather x1 -> x0, waiting for transfers between devices: 27.5 us -> none  [on_device(): panel_piece = lax.all_gather(stripe_panel, 'col', axis=0, tiled=True)]
    all_gather x1 -> x0, blocking collectives: 26.1 us -> none  [on_device(): gathered = lax.all_gather(projected, ('enc', 'row'), axis=0, tiled=True)]
    gather x5 -> x0, local copies, waits for them, and re-layouts: 19.3 us -> none  [the longest x1 10.6 us: on_device(): jnp.take_along_axis(partials.reshape(row_devices, seg_rows, half_width),...]
    dot_general x9 -> x0, matrix products: 16.9 us -> none  [the longest x1 3.5 us: aggregate_slots(): jnp.einsum('lr,lif->rif', row_pick, products, precision=lax.Precision.HIG...]
    scatter-add x1 -> x0, other arithmetic: 9.99 us -> none  [place_terms(): placed = placed.at[local].add(products, mode='drop')]
  transfers between devices with their start and end apart: 4 -> 0, of which waited for: 4 -> 0; matrix products, arithmetic and copies ran while one was open for 2% -> 0% of each run, Pallas kernels for 0% -> 0%
where the time goes in v1:
time: 66.4 us; the launch traced here: 66 us
  Pallas kernels  52.3 us (79%)
  local copies, waits for them, and re-layouts  10.3 us (16%)
  other arithmetic  2.19 us (3%)
  between operations  1.32 us (2%)
    pallas_call x1, Pallas kernels, on_device(): pl.pallas_call(functools.partial(kernel, n_row, n_col), out_shape=(jax.Sh...  52.3 us
    unnamed x20, local copies, waits for them, and re-layouts  9.66 us

profile of v1, /device:TPU:0, one launch (start us, length us, event | category | flops | bytes accessed | tf_op | source)
XLA Modules:
  0.0 66.0 jit_solution(10167858157473117176)
XLA Ops:
  1.3 0.5 broadcast.36
  1.8 1.3 %reduce.11 = s32[48]{0:T(128)S(1)} reduce(s32[1,48]{1,0:T(1,128)} %param.17, s32[]{:T(128)} %broadcast.36), dimensions={0}, to_apply=%param.17.reduce_sub_computation.3 | reduce | bytes 388 | tf_op args[5]
  3.1 0.7 %multiply_reduce_fusion = (s32[48]{0:T(128)S(1)}, s32[48]{0:T(128)S(1)}) fusion(s32[1,48]{1,0:T(1,128)} %param.19, s32[1,48]{1,0:T(1,128)} %param.18), kind=kLoop, calls=%fused_computation.5 | loop fusion | flops 96 | bytes 768 | tf_op jit(solution)/shard_map/mul | solution.py:302
  3.8 0.1 mul.41
  3.9 0.1 eq.15
  4.0 0.1 copy.15
  4.0 0.1 mul.38
  4.2 0.1 copy.16
  4.2 0.2 select_reduce_fusion
  4.4 0.1 copy.17
  4.5 0.1 reshape.38.meta
  4.6 0.0 copy-start
  4.6 1.4 %copy-done = bf16[1,48,128,128]{3,2,1,0:T(8,128)(2,1)S(1)} copy-done((bf16[1,48,128,128]{3,2,1,0:T(8,128)(2,1)S(1)}, bf16[1,48,128,128]{3,2,1,0:T(8,128)(2,1)}, u32[]{:S(2)}) %copy-start) | copy-done | bytes 1572888
  6.0 0.0 copy-start.1
  6.0 0.9 %copy-done.1 = bf16[256,256]{1,0:T(8,128)(2,1)S(1)} copy-done((bf16[256,256]{1,0:T(8,128)(2,1)S(1)}, bf16[256,256]{1,0:T(8,128)(2,1)}, u32[]{:S(2)}) %copy-start.1) | copy-done | bytes 131096
  6.9 0.0 copy-start.2
  6.9 0.9 %copy-done.2 = bf16[256,256]{1,0:T(8,128)(2,1)S(1)} copy-done((bf16[256,256]{1,0:T(8,128)(2,1)S(1)}, bf16[256,256]{1,0:T(8,128)(2,1)}, u32[]{:S(2)}) %copy-start.2) | copy-done | bytes 131096
  7.8 0.0 copy-start.3
  7.8 0.9 %copy-done.3 = bf16[256,256]{1,0:T(8,128)(2,1)S(1)} copy-done((bf16[256,256]{1,0:T(8,128)(2,1)S(1)}, bf16[256,256]{1,0:T(8,128)(2,1)}, u32[]{:S(2)}) %copy-start.3) | copy-done | bytes 131096
  8.7 0.0 copy-start.4
  8.7 0.8 %copy-done.4 = bf16[1,128,256]{2,1,0:T(8,128)(2,1)S(1)} copy-done((bf16[1,128,256]{2,1,0:T(8,128)(2,1)S(1)}, bf16[1,128,256]{2,1,0:T(8,128)(2,1)}, u32[]{:S(2)}) %copy-start.4) | copy-done | bytes 65560
  9.6 0.0 copy-start.5
  9.6 0.8 %copy-done.5 = bf16[1,256,128]{2,1,0:T(8,128)(2,1)S(1)} copy-done((bf16[1,256,128]{2,1,0:T(8,128)(2,1)S(1)}, bf16[1,256,128]{2,1,0:T(8,128)(2,1)}, u32[]{:S(2)}) %copy-start.5) | copy-done | bytes 65560
  10.4 0.0 copy-start.6
  10.4 0.7 %copy-done.6 = s32[4,1,256]{2,1,0:T(1,128)S(1)} copy-done((s32[4,1,256]{2,1,0:T(1,128)S(1)}, s32[4,1,256]{2,1,0:T(1,128)}, u32[]{:S(2)}) %copy-start.6) | copy-done | bytes 4120
  11.1 0.0 copy-start.7
  11.1 0.7 %copy-done.7 = f32[256]{0:T(256)S(1)} copy-done((f32[256]{0:T(256)S(1)}, f32[256]{0:T(256)}, u32[]{:S(2)}) %copy-start.7) | copy-done | bytes 1048
  11.8 52.3 %shard_map.139 = (bf16[256,128]{1,0:T(8,128)(2,1)S(1)}, f32[256,256]{1,0:T(8,128)S(1)}, f32[128,256]{1,0:T(8,128)S(1)}) custom-call(bf16[128,256]{1,0:T(8,128)(2,1)S(1)} %bitcast.10, bf16[256,256]{1,0:T(8,128)(2,1)S(1)} %copy-done.1, f32[1,256]{1,0:T(1,128)S(1)} %bitcast.13, bf16[256,256]{1,0:T(8,128)(2,1)S(1)} %copy-done.2, bf16[256,256]{1,0:T(8,128)(2,1)S(1)} %copy-done.3, ...), custom_call_target="tpu_custom_call" | custom-call | tf_op jit(solution)/shard_map/pallas_call | solution.py:336
  64.0 0.6 copy.22
  64.7 0.7 %copy.23 = f32[256,256]{1,0:T(8,128)} copy(f32[256,256]{1,0:T(8,128)S(1)} %get-tuple-element.15) | data formatting | bytes 524288
  65.4 0.7 copy.24
  (1 shorter events, 0.0 us)
Async XLA Ops:
  4.6 1.4 %copy-start = (bf16[1,48,128,128]{3,2,1,0:T(8,128)(2,1)S(1)}, bf16[1,48,128,128]{3,2,1,0:T(8,128)(2,1)}, u32[]{:S(2)}) copy-start(bf16[1,48,128,128]{3,2,1,0:T(8,128)(2,1)} %param.21) | copy-start | bytes 4718596
  6.0 0.9 %copy-start.1 = (bf16[256,256]{1,0:T(8,128)(2,1)S(1)}, bf16[256,256]{1,0:T(8,128)(2,1)}, u32[]{:S(2)}) copy-start(bf16[256,256]{1,0:T(8,128)(2,1)} %w1.1) | copy-start | bytes 393220
  6.9 0.9 %copy-start.2 = (bf16[256,256]{1,0:T(8,128)(2,1)S(1)}, bf16[256,256]{1,0:T(8,128)(2,1)}, u32[]{:S(2)}) copy-start(bf16[256,256]{1,0:T(8,128)(2,1)} %w2.1) | copy-start | bytes 393220
  7.8 0.9 %copy-start.3 = (bf16[256,256]{1,0:T(8,128)(2,1)S(1)}, bf16[256,256]{1,0:T(8,128)(2,1)}, u32[]{:S(2)}) copy-start(bf16[256,256]{1,0:T(8,128)(2,1)} %wl.1) | copy-start | bytes 393220
  8.7 0.8 %copy-start.4 = (bf16[1,128,256]{2,1,0:T(8,128)(2,1)S(1)}, bf16[1,128,256]{2,1,0:T(8,128)(2,1)}, u32[]{:S(2)}) copy-start(bf16[1,128,256]{2,1,0:T(8,128)(2,1)} %param.12) | copy-start | bytes 196612
  9.6 0.8 %copy-start.5 = (bf16[1,256,128]{2,1,0:T(8,128)(2,1)S(1)}, bf16[1,256,128]{2,1,0:T(8,128)(2,1)}, u32[]{:S(2)}) copy-start(bf16[1,256,128]{2,1,0:T(8,128)(2,1)} %param.23) | copy-start | bytes 196612
  10.4 0.7 %copy-start.6 = (s32[4,1,256]{2,1,0:T(1,128)S(1)}, s32[4,1,256]{2,1,0:T(1,128)}, u32[]{:S(2)}) copy-start(s32[4,1,256]{2,1,0:T(1,128)} %order.1) | copy-start | bytes 12292
  11.1 0.7 %copy-start.7 = (f32[256]{0:T(256)S(1)}, f32[256]{0:T(256)}, u32[]{:S(2)}) copy-start(f32[256]{0:T(256)} %param.14) | copy-start | bytes 3076

commit v2 on v1

--- a/solution.py
+++ b/solution.py
@@ -22,8 +22,9 @@
     return lax.dot_general(a, b, (((ca,), (cb,)), ((), ())), preferred_element_type=F32)
 
 
-def kernel(n_row, n_col, emb, w1, b1, w2, wl, meta, tiles, order, cot,
+def kernel(n_row, n_col, emb_h, w1_h, b1_h, w2_h, wl_h, src, rws, cls, cnt, tiles_h, order_h, cot_h,
            act_o, gl_o, ge_o,
+           emb, w1, b1, w2, wl, tiles, order, cot, meta, in_sem,
            first, pall, psend, eall, pgx, pgsend, feat, acc, pgt, pb, rb, sb, cb, own,
            glp, glr, glc, glf,
            m_send, m_recv, fc_send, fr_send, f_recv, br_send, br_recv, bc_send, bc_recv,
@@ -48,6 +49,12 @@
             src_ref=src, dst_ref=dst, send_sem=ssem, recv_sem=rsem,
             device_id=dev, device_id_type=MESH)
 
+    pairs = [(emb_h, emb), (w1_h, w1), (b1_h, b1), (w2_h, w2), (wl_h, wl), (order_h, order),
+             (tiles_h, tiles), (cot_h, cot)]
+    loads = [pltpu.make_async_copy(a, b, in_sem.at[i]) for i, (a, b) in enumerate(pairs)]
+    for load in loads:
+        load.start()
+
     barrier = pltpu.get_barrier_semaphore()
     pl.semaphore_signal(barrier, inc=1, device_id={"enc": mate}, device_id_type=MESH)
     for d in range(1, n_row):
@@ -57,6 +64,25 @@
     for d in range(1, n_col):
         pl.semaphore_signal(barrier, inc=1, device_id={"col": col_of(d)}, device_id_type=MESH)
 
+    runs = src.shape[1] // PAIR
+
+    def tabulate(seg, carry):
+        at = jnp.int32(0)
+        there = jnp.int32(0)
+        for j in range(runs):
+            hit = src[0, j * PAIR] == seg
+            at = jnp.where(hit, j * PAIR, at)
+            there = jnp.where(hit, 1, there)
+        for k in range(PAIR):
+            slot = at + k
+            live = jnp.where(slot < cnt[0], there, 0)
+            meta[seg * PAIR + k] = live + rws[0, slot] * 2 + cls[0, slot] * 4 + slot * 8
+        return carry
+
+    lax.fori_loop(0, n_row * n_col, tabulate, 0)
+
+    for load in loads[:6]:
+        load.wait()
     linear = dot(emb[...], w1[...]) + b1[...]
     first[...] = linear
     hidden = (linear * jax.nn.sigmoid(linear)).astype(BF16)
@@ -124,6 +150,7 @@
             rhs.append(pick([feat[seg, b] for b in range(rows // ts)], c))
         return dot(jnp.concatenate(lhs, axis=1), jnp.concatenate(rhs, axis=0))
 
+    loads[6].wait()
     acc[...] = forward(me_slot)
 
     def relay(dc, carry):
@@ -146,6 +173,7 @@
 
     lax.fori_loop(0, n_col * (n_row - 1), take, 0)
 
+    loads[7].wait()
     aggregated = acc[...]
     sig = jax.nn.sigmoid(aggregated)
     act_o[...] = (aggregated * sig).astype(BF16)
@@ -295,20 +323,23 @@
     width = full // 2
     ts = block_tiles.shape[-1]
     blocks = rows // ts
-    total = block_source.shape[1]
-
-    slot = jnp.arange(total, dtype=jnp.int32)
-    live = (slot < block_count[0]).astype(jnp.int32)
-    value = (live + block_rows[0] * 2 + block_cols[0] * 4 + slot * 8).reshape(-1, PAIR)
-    sources = block_source[0].reshape(-1, PAIR)
-    match = sources[None, :, :] == jnp.arange(segs, dtype=jnp.int32)[:, None, None]
-    meta = jnp.sum(jnp.where(match, value[None], 0), axis=1).reshape(segs * PAIR)
-
+    total = block_tiles.shape[1]
     vmem = pl.BlockSpec(memory_space=pltpu.VMEM)
+    hbm = pl.BlockSpec(memory_space=pltpu.HBM)
     smem = pl.BlockSpec(memory_space=pltpu.SMEM)
     dma = pltpu.SemaphoreType.DMA
     chunk = full // n_row
     scratch = [
+        pltpu.VMEM((half, full), BF16),
+        pltpu.VMEM((full, full), BF16),
+        pltpu.VMEM((1, full), F32),
+        pltpu.VMEM((full, full), BF16),
+        pltpu.VMEM((full, full), BF16),
+        pltpu.VMEM((total, ts, ts), BF16),
+        pltpu.VMEM(node_order.shape, jnp.int32),
+        pltpu.VMEM((rows, width), BF16),
+        pltpu.SMEM((segs * PAIR,), jnp.int32),
+        dma((8,)),
         pltpu.VMEM((half, full), F32),
         pltpu.VMEM((2, half, width), BF16),
         pltpu.VMEM((2, half, width), BF16),
@@ -340,13 +371,13 @@
             jax.ShapeDtypeStruct((full, full), F32),
             jax.ShapeDtypeStruct((half, full), F32),
         ),
-        in_specs=[vmem, vmem, vmem, vmem, vmem, smem, vmem, vmem, vmem],
+        in_specs=[hbm] * 5 + [smem] * 4 + [hbm] * 3,
         out_specs=(vmem, vmem, vmem),
         scratch_shapes=scratch,
         compiler_params=pltpu.CompilerParams(
-            collective_id=0, has_side_effects=True, vmem_limit_bytes=48 * 1024 * 1024),
-    )(embedding[0], w_first, b_first[None], w_second, w_layer, meta, block_tiles[0],
-      node_order, cotangent[0])
+            collective_id=0, has_side_effects=True, vmem_limit_bytes=64 * 1024 * 1024),
+    )(embedding[0], w_first, b_first[None], w_second, w_layer, block_source,
+      block_rows, block_cols, block_count, block_tiles[0], node_order, cotangent[0])
     return (activated[None], grad_layer, grad_embed[None])
 
 

time: 66.4 us -> 59.7 us (0.90)
  local copies, waits for them, and re-layouts: 10.3 us -> 4.71 us
  other arithmetic: 2.19 us -> 0 us
  Pallas kernels: 52.3 us -> 53.5 us
    unnamed x20 -> x3, local copies, waits for them, and re-layouts: 9.66 us -> 4.71 us
    unnamed x1 -> x0, other arithmetic: 1.32 us -> none
    pallas_call x1, Pallas kernels: 52.3 us -> 53.5 us  [on_device(): pl.pallas_call(functools.partial(kernel, n_row, n_col), out_shape=(jax.Sh...]
    mul x1 -> x0, other arithmetic: 0.69 us -> none  [on_device(): block_cols[0] * 4]
where the time goes in v2:
time: 59.7 us; the launch traced here: 59.5 us
  Pallas kernels  53.5 us (90%)
  local copies, waits for them, and re-layouts  4.71 us (8%)
  between operations  1.29 us (2%)
    pallas_call x1, Pallas kernels, on_device(): pl.pallas_call(functools.partial(kernel, n_row, n_col), out_shape=(jax.Sh...  53.5 us
    unnamed x3, local copies, waits for them, and re-layouts  4.71 us

profile of v2, /device:TPU:0, one launch (start us, length us, event | category | flops | bytes accessed | tf_op | source)
XLA Modules:
  0.0 59.5 jit_solution(334316412266303938)
XLA Ops:
  1.3 53.5 %shard_map.139 = (bf16[256,128]{1,0:T(8,128)(2,1)}, f32[256,256]{1,0:T(8,128)}, f32[128,256]{1,0:T(8,128)}) custom-call(bf16[128,256]{1,0:T(8,128)(2,1)} %bitcast.8, bf16[256,256]{1,0:T(8,128)(2,1)} %w1_h.1, f32[1,256]{1,0:T(1,128)} %bitcast.11, bf16[256,256]{1,0:T(8,128)(2,1)} %w2_h.1, bf16[256,256]{1,0:T(8,128)(2,1)} %wl_h.1, s32[1,48]{1,0:T(1,128)} %src.1, ...), custom_call_target="tpu_custom_call" | custom-call | tf_op jit(solution)/shard_map/pallas_call | solution.py:367
  54.7 1.5 %copy.19 = bf16[1,256,128]{2,1,0:T(8,128)(2,1)} copy(bf16[1,256,128]{2,1,0:T(8,128)(2,1)} %bitcast.10) | data formatting | bytes 131072
  56.2 1.7 %copy.20 = f32[256,256]{1,0:T(8,128)} copy(f32[256,256]{1,0:T(8,128)} %get-tuple-element.13) | data formatting | bytes 524288
  57.9 1.6 %copy.21 = f32[1,128,256]{2,1,0:T(8,128)} copy(f32[1,128,256]{2,1,0:T(8,128)} %bitcast.7) | data formatting | bytes 262144

commit v3 on v2

--- a/solution.py
+++ b/solution.py
@@ -23,7 +23,8 @@
 
 
 def kernel(n_row, n_col, emb_h, w1_h, b1_h, w2_h, wl_h, src, rws, cls, cnt, tiles_h, order_h, cot_h,
-           act_o, gl_o, ge_o,
+           act_h, gl_h, ge_h,
+           act_o, gl_o, ge_o, out_sem,
            emb, w1, b1, w2, wl, tiles, order, cot, meta, in_sem,
            first, pall, psend, eall, pgx, pgsend, feat, acc, pgt, pb, rb, sb, cb, own,
            glp, glr, glc, glf,
@@ -106,22 +107,29 @@
     grid_own = dot(perm_t, pall[...].reshape(rows, width), 0, 0).astype(BF16)
     feat[me_slot] = grid_own.reshape(rows // ts, ts, width)
 
-    def feat_col(d):
-        slot = me_r * n_col + me_c
-        return remote(feat.at[slot], feat.at[slot], fc_send.at[d], f_recv.at[slot], col=col_of(d))
+    def feat_col(c, step):
+        slot = me_r * n_col + c
+        return remote(feat.at[slot], feat.at[slot], fc_send.at[(step + 1) // 2 * n_col + c],
+                      f_recv.at[slot], col=lax.rem(me_c + step + n_col, n_col))
 
     def feat_row(dc, dr):
-        slot = me_r * n_col + col_of(dc)
+        slot = me_r * n_col + dc
         return remote(feat.at[slot], feat.at[slot], fr_send.at[dc * n_row + dr],
                       f_recv.at[slot], row=row_of(dr))
 
     def feat_wait(slot):
         remote(feat.at[slot], feat.at[slot], fc_send.at[0], f_recv.at[slot], enc=mate).wait_recv()
 
-    for d in range(1, n_col):
-        feat_col(d).start()
+    @pl.when(me_c < n_col - 1)
+    def _():
+        feat_col(me_c, 1).start()
+
+    @pl.when(me_c > 0)
+    def _():
+        feat_col(me_c, -1).start()
+
     for d in range(1, n_row):
-        feat_row(0, d).start()
+        feat_row(me_c, d).start()
 
     def slots(seg):
         out = []
@@ -153,20 +161,54 @@
     loads[6].wait()
     acc[...] = forward(me_slot)
 
-    def relay(dc, carry):
-        slot = me_r * n_col + col_of(dc)
-        feat_wait(slot)
-        for d in range(1, n_row):
-            feat_row(dc, d).start()
-        acc[...] += forward(slot)
+    def relay(d, carry):
+        left = me_c - d
+        right = me_c + d
+
+        @pl.when(left >= 0)
+        def _():
+            feat_wait(me_r * n_col + left)
+
+            @pl.when(me_c < n_col - 1)
+            def _():
+                feat_col(left, 1).start()
+
+            for dr in range(1, n_row):
+                feat_row(left, dr).start()
+
+        @pl.when(right < n_col)
+        def _():
+            feat_wait(me_r * n_col + right)
+
+            @pl.when(me_c > 0)
+            def _():
+                feat_col(right, -1).start()
+
+            for dr in range(1, n_row):
+                feat_row(right, dr).start()
+
+        @pl.when(left >= 0)
+        def _():
+            acc[...] += forward(me_r * n_col + left)
+
+        @pl.when(right < n_col)
+        def _():
+            acc[...] += forward(me_r * n_col + right)
+
         return carry
 
     lax.fori_loop(1, n_col, relay, 0)
 
+    def nearest(k):
+        low = jnp.minimum(me_c, n_col - 1 - me_c)
+        d = (k + 1) // 2
+        near = jnp.where(k % 2 == 1, me_c - d, me_c + d)
+        far = jnp.where(me_c > n_col - 1 - me_c, n_col - 1 - k, k)
+        return jnp.where(k <= 2 * low, near, far)
+
     def take(step, carry):
-        dc = step // (n_row - 1)
         dr = step % (n_row - 1) + 1
-        slot = row_of(dr) * n_col + col_of(dc)
+        slot = row_of(dr) * n_col + nearest(step // (n_row - 1))
         feat_wait(slot)
         acc[...] += forward(slot)
         return carry
@@ -177,6 +219,8 @@
     aggregated = acc[...]
     sig = jax.nn.sigmoid(aggregated)
     act_o[...] = (aggregated * sig).astype(BF16)
+    act_copy = pltpu.make_async_copy(act_o, act_h, out_sem.at[0])
+    act_copy.start()
     slope = sig * (1.0 + aggregated * (1.0 - sig))
     pre = cot[...].astype(F32) * slope
     for b in range(rows // ts):
@@ -256,6 +300,8 @@
     encoded_grad = dot(full_grad, wl[...], 1, 1).astype(BF16)
     hidden_grad = (dot(encoded_grad, w2[...], 1, 1) * silu_slope(first[...])).astype(BF16)
     ge_o[...] = dot(hidden_grad, w1[...], 1, 1)
+    ge_copy = pltpu.make_async_copy(ge_o, ge_h, out_sem.at[2])
+    ge_copy.start()
 
     total = glp[me_r].astype(F32)
     for d in range(1, n_row):
@@ -292,9 +338,21 @@
         for r in range(n_row):
             gl_o[r * chunk:(r + 1) * chunk, e * width:(e + 1) * width] = (
                 glf[e * n_row + r].astype(F32))
+    gl_copy = pltpu.make_async_copy(gl_o, gl_h, out_sem.at[1])
+    gl_copy.start()
+    act_copy.wait()
+    ge_copy.wait()
+
+    for c in range(n_col):
+        @pl.when(jnp.logical_and(c <= me_c, me_c < n_col - 1))
+        def _():
+            feat_col(c, 1).wait_send()
+
+        @pl.when(jnp.logical_and(c >= me_c, me_c > 0))
+        def _():
+            feat_col(c, -1).wait_send()
 
     for d in range(1, n_col):
-        feat_col(d).wait_send()
         back_col(d).wait_send()
         gl_col(d).wait_send()
     for d in range(1, n_row):
@@ -310,6 +368,20 @@
         return carry
 
     lax.fori_loop(0, n_col * (n_row - 1), drain, 0)
+    gl_copy.wait()
+
+
+def hand_out(a, b, c, a_out, b_out, c_out, a_mid, b_mid, c_mid, in_sem, out_sem):
+    ways = [(a, a_mid, a_out), (b, b_mid, b_out), (c, c_mid, c_out)]
+    ins = [pltpu.make_async_copy(x, y, in_sem.at[i]) for i, (x, y, _) in enumerate(ways)]
+    outs = [pltpu.make_async_copy(y, z, out_sem.at[i]) for i, (_, y, z) in enumerate(ways)]
+    for copy in ins:
+        copy.start()
+    for before, after in zip(ins, outs):
+        before.wait()
+        after.start()
+    for copy in outs:
+        copy.wait()
 
 
 def on_device(embedding, w_first, b_first, w_second, w_layer, block_source, block_rows,
@@ -324,12 +396,15 @@
     ts = block_tiles.shape[-1]
     blocks = rows // ts
     total = block_tiles.shape[1]
-    vmem = pl.BlockSpec(memory_space=pltpu.VMEM)
     hbm = pl.BlockSpec(memory_space=pltpu.HBM)
     smem = pl.BlockSpec(memory_space=pltpu.SMEM)
     dma = pltpu.SemaphoreType.DMA
     chunk = full // n_row
     scratch = [
+        pltpu.VMEM((rows, width), BF16),
+        pltpu.VMEM((full, full), F32),
+        pltpu.VMEM((half, full), F32),
+        dma((3,)),
         pltpu.VMEM((half, full), BF16),
         pltpu.VMEM((full, full), BF16),
         pltpu.VMEM((1, full), F32),
@@ -359,25 +434,34 @@
         pltpu.VMEM((n_col, chunk, width), BF16),
         pltpu.VMEM((2 * n_row, chunk, width), BF16),
         dma((3,)), dma((3,)),
-        dma((n_col,)), dma((segs,)), dma((segs,)),
+        dma((2 * n_col,)), dma((segs,)), dma((segs,)),
         dma((segs,)), dma((segs,)), dma((n_col,)), dma((n_col,)),
         dma((n_row,)), dma((n_row,)), dma((n_col,)), dma((n_col,)),
         dma((2 * n_row,)), dma((2 * n_row,)),
     ]
-    activated, grad_layer, grad_embed = pl.pallas_call(
+    shapes = (
+        jax.ShapeDtypeStruct((rows, width), BF16),
+        jax.ShapeDtypeStruct((full, full), F32),
+        jax.ShapeDtypeStruct((half, full), F32),
+    )
+    results = pl.pallas_call(
         functools.partial(kernel, n_row, n_col),
-        out_shape=(
-            jax.ShapeDtypeStruct((rows, width), BF16),
-            jax.ShapeDtypeStruct((full, full), F32),
-            jax.ShapeDtypeStruct((half, full), F32),
-        ),
+        out_shape=shapes,
         in_specs=[hbm] * 5 + [smem] * 4 + [hbm] * 3,
-        out_specs=(vmem, vmem, vmem),
+        out_specs=(hbm, hbm, hbm),
         scratch_shapes=scratch,
         compiler_params=pltpu.CompilerParams(
             collective_id=0, has_side_effects=True, vmem_limit_bytes=64 * 1024 * 1024),
     )(embedding[0], w_first, b_first[None], w_second, w_layer, block_source,
       block_rows, block_cols, block_count, block_tiles[0], node_order, cotangent[0])
+    activated, grad_layer, grad_embed = pl.pallas_call(
+        hand_out,
+        out_shape=shapes,
+        in_specs=[hbm] * 3,
+        out_specs=(hbm, hbm, hbm),
+        scratch_shapes=[pltpu.VMEM(x.shape, x.dtype) for x in shapes] + [dma((3,)), dma((3,))],
+        compiler_params=pltpu.CompilerParams(vmem_limit_bytes=64 * 1024 * 1024),
+    )(*results)
     return (activated[None], grad_layer, grad_embed[None])
 
 

time: 59.7 us -> 53.2 us (0.89)
  local copies, waits for them, and re-layouts: 4.71 us -> 0 us
  Pallas kernels: 53.5 us -> 51.7 us
    unnamed x3 -> x0, local copies, waits for them, and re-layouts: 4.71 us -> none
    pallas_call x1 -> x2, Pallas kernels: 53.5 us -> 51.7 us  [the longest x1 49.9 us: on_device(): pl.pallas_call(functools.partial(kernel, n_row, n_col), out_shape=shapes,...]
where the time goes in v3:
time: 53.2 us; the launch traced here: 53 us
  Pallas kernels  51.7 us (97%)
  between operations  1.29 us (2%)
    pallas_call x1, Pallas kernels, on_device(): pl.pallas_call(functools.partial(kernel, n_row, n_col), out_shape=shapes,...  49.9 us
    pallas_call x1, Pallas kernels, on_device(): pl.pallas_call(hand_out, out_shape=shapes, in_specs=[hbm] * 3, out_specs=...  1.78 us

profile of v3, /device:TPU:0, one launch (start us, length us, event | category | flops | bytes accessed | tf_op | source)
XLA Modules:
  0.0 53.0 jit_solution(9957352802431481917)
XLA Ops:
  1.3 49.9 %shard_map.139 = (bf16[256,128]{1,0:T(8,128)(2,1)}, f32[256,256]{1,0:T(8,128)}, f32[128,256]{1,0:T(8,128)}) custom-call(bf16[128,256]{1,0:T(8,128)(2,1)} %bitcast.7, bf16[256,256]{1,0:T(8,128)(2,1)} %w1_h.1, f32[1,256]{1,0:T(1,128)} %bitcast.9, bf16[256,256]{1,0:T(8,128)(2,1)} %w2_h.1, bf16[256,256]{1,0:T(8,128)(2,1)} %wl_h.1, s32[1,48]{1,0:T(1,128)} %src.1, ...), custom_call_target="tpu_custom_call" | custom-call | tf_op jit(solution)/shard_map/pallas_call | solution.py:447
  51.2 1.8 %shard_map.140 = (bf16[256,128]{1,0:T(8,128)(2,1)}, f32[256,256]{1,0:T(8,128)}, f32[128,256]{1,0:T(8,128)}) custom-call(bf16[256,128]{1,0:T(8,128)(2,1)} %get-tuple-element.9.a, f32[256,256]{1,0:T(8,128)} %get-tuple-element.10.b, f32[128,256]{1,0:T(8,128)} %get-tuple-element.11.c), custom_call_target="tpu_custom_call" | custom-call | tf_op jit(solution)/shard_map/pallas_call | solution.py:457

commit v4 on v3

--- a/solution.py
+++ b/solution.py
@@ -22,10 +22,10 @@
     return lax.dot_general(a, b, (((ca,), (cb,)), ((), ())), preferred_element_type=F32)
 
 
-def kernel(n_row, n_col, emb_h, w1_h, b1_h, w2_h, wl_h, src, rws, cls, cnt, tiles_h, order_h, cot_h,
+def kernel(n_row, n_col, emb_h, w1_h, b1_h, w2_h, wl_h, src_h, rws_h, cls_h, cnt, tiles_h, order_h, cot_h,
            act_h, gl_h, ge_h,
            act_o, gl_o, ge_o, out_sem,
-           emb, w1, b1, w2, wl, tiles, order, cot, meta, in_sem,
+           emb, w1, b1, w2, wl, tiles, order, cot, src, rws, cls, meta, in_sem,
            first, pall, psend, eall, pgx, pgsend, feat, acc, pgt, pb, rb, sb, cb, own,
            glp, glr, glc, glf,
            m_send, m_recv, fc_send, fr_send, f_recv, br_send, br_recv, bc_send, bc_recv,
@@ -51,9 +51,9 @@
             device_id=dev, device_id_type=MESH)
 
     pairs = [(emb_h, emb), (w1_h, w1), (b1_h, b1), (w2_h, w2), (wl_h, wl), (order_h, order),
-             (tiles_h, tiles), (cot_h, cot)]
+             (tiles_h, tiles), (cot_h, cot), (src_h, src), (rws_h, rws), (cls_h, cls)]
     loads = [pltpu.make_async_copy(a, b, in_sem.at[i]) for i, (a, b) in enumerate(pairs)]
-    for load in loads:
+    for load in loads[8:] + loads[:8]:
         load.start()
 
     barrier = pltpu.get_barrier_semaphore()
@@ -80,6 +80,8 @@
             meta[seg * PAIR + k] = live + rws[0, slot] * 2 + cls[0, slot] * 4 + slot * 8
         return carry
 
+    for load in loads[8:]:
+        load.wait()
     lax.fori_loop(0, n_row * n_col, tabulate, 0)
 
     for load in loads[:6]:
@@ -239,8 +241,11 @@
         return remote(pb.at[slot], rb.at[there], br_send.at[dc * n_row + dr],
                       br_recv.at[there], row=row_of(dr))
 
+    def farthest(k):
+        return lax.rem(nearest(n_col - 1 - k) - me_c + n_col, n_col)
+
     def give(step, carry):
-        dc = lax.rem(step // (n_row - 1) + 1, n_col)
+        dc = farthest(step // (n_row - 1))
         dr = step % (n_row - 1) + 1
         slot = row_of(dr) * n_col + col_of(dc)
         pb[slot] = backward(slot).astype(BF16)
@@ -260,12 +265,13 @@
     def back_col(dc):
         return remote(sb.at[dc], cb.at[me_c], bc_send.at[dc], bc_recv.at[me_c], col=col_of(dc))
 
-    def pass_on(dc, carry):
+    def pass_on(k, carry):
+        dc = farthest(k)
         sb[dc] = row_total(dc).astype(BF16)
         back_col(dc).start()
         return carry
 
-    lax.fori_loop(1, n_col, pass_on, 0)
+    lax.fori_loop(0, n_col - 1, pass_on, 0)
     own[...] = row_total(0)
 
     def collect(dc, carry):
@@ -413,8 +419,11 @@
         pltpu.VMEM((total, ts, ts), BF16),
         pltpu.VMEM(node_order.shape, jnp.int32),
         pltpu.VMEM((rows, width), BF16),
+        pltpu.SMEM((1, total), jnp.int32),
+        pltpu.SMEM((1, total), jnp.int32),
+        pltpu.SMEM((1, total), jnp.int32),
         pltpu.SMEM((segs * PAIR,), jnp.int32),
-        dma((8,)),
+        dma((11,)),
         pltpu.VMEM((half, full), F32),
         pltpu.VMEM((2, half, width), BF16),
         pltpu.VMEM((2, half, width), BF16),
@@ -447,7 +456,7 @@
     results = pl.pallas_call(
         functools.partial(kernel, n_row, n_col),
         out_shape=shapes,
-        in_specs=[hbm] * 5 + [smem] * 4 + [hbm] * 3,
+        in_specs=[hbm] * 8 + [smem] + [hbm] * 3,
         out_specs=(hbm, hbm, hbm),
         scratch_shapes=scratch,
         compiler_params=pltpu.CompilerParams(

time: 53.2 us -> 51.2 us (0.962)
  Pallas kernels: 51.7 us -> 49.8 us
    pallas_call x1, Pallas kernels: 49.9 us -> 48 us  [on_device(): pl.pallas_call(functools.partial(kernel, n_row, n_col), out_shape=shapes,...]
where the time goes in v4:
time: 51.2 us; the launch traced here: 51 us
  Pallas kernels  49.8 us (97%)
  between operations  1.29 us (3%)
    pallas_call x1, Pallas kernels, on_device(): pl.pallas_call(functools.partial(kernel, n_row, n_col), out_shape=shapes,...  48 us
    pallas_call x1, Pallas kernels, on_device(): pl.pallas_call(hand_out, out_shape=shapes, in_specs=[hbm] * 3, out_specs=...  1.78 us

profile of v4, /device:TPU:0, one launch (start us, length us, event | category | flops | bytes accessed | tf_op | source)
XLA Modules:
  0.0 51.0 jit_solution(5914563018336642197)
XLA Ops:
  1.3 48.0 %shard_map.139 = (bf16[256,128]{1,0:T(8,128)(2,1)}, f32[256,256]{1,0:T(8,128)}, f32[128,256]{1,0:T(8,128)}) custom-call(bf16[128,256]{1,0:T(8,128)(2,1)} %bitcast.7, bf16[256,256]{1,0:T(8,128)(2,1)} %w1_h.1, f32[1,256]{1,0:T(1,128)} %bitcast.9, bf16[256,256]{1,0:T(8,128)(2,1)} %w2_h.1, bf16[256,256]{1,0:T(8,128)(2,1)} %wl_h.1, s32[1,48]{1,0:T(1,128)} %src_h.1, ...), custom_call_target="tpu_custom_call" | custom-call | tf_op jit(solution)/shard_map/pallas_call | solution.py:456
  49.3 1.8 %shard_map.140 = (bf16[256,128]{1,0:T(8,128)(2,1)}, f32[256,256]{1,0:T(8,128)}, f32[128,256]{1,0:T(8,128)}) custom-call(bf16[256,128]{1,0:T(8,128)(2,1)} %get-tuple-element.9.a, f32[256,256]{1,0:T(8,128)} %get-tuple-element.10.b, f32[128,256]{1,0:T(8,128)} %get-tuple-element.11.c), custom_call_target="tpu_custom_call" | custom-call | tf_op jit(solution)/shard_map/pallas_call | solution.py:466
